TPU v7x, 256 devices: a whole 4x4x8 slice. The times are simulated.
256 devices in a mesh: blk: 16 (over x_lo, z), rep: 16 (over y, x_hi, core).
Axes of the slice: x: 4 (x_hi: 2, x_lo: 2; x = x_hi * 2 + x_lo), y: 4, z: 8, core: 2. Of those that a mesh axis runs over, the one named last changes fastest.
Arguments:
- a_blocks: bfloat16 [48, 16, 6, 128, 128], P('blk', None, None, None, 'rep'), may hold values from -0.5 to 0.5
- a_cols: int32 [48, 16, 6], P('blk'), may hold values from 0 to 111, as said below
- b_blocks: bfloat16 [1792, 16, 3, 128, 128], P('blk', 'rep'), may hold values from -6 to 6
- b_cols: int32 [1792, 16, 3], P('blk', 'rep'), may hold values from 0 to 111, as said below
- c_cols: int32 [48, 16, 4], P(None, 'rep'), may hold values from 0 to 111, as said below
Outputs:
- c_blocks: float32 [48, 16, 4, 128, 128], P('blk', 'rep')
Inputs may be any that keep to these rules, and one draw needn't show every extreme that they name: `a_cols`: within each block row and panel the 6 entries are distinct. `b_cols`: within each block row and tile the 3 entries are distinct. `c_cols`: within each block row and tile the 4 entries are distinct.
All inputs are finite; a program needn't handle non-finite values.
Results may differ from a plain program's by a relative error of at most 0.0003.
Values may be sent and summed in bfloat16 or wider, within the bound.
A program may use at most 128 MiB of HBM per device.

v0:
```python
import math

import jax
import jax.numpy as jnp
from jax import lax
from jax.sharding import PartitionSpec as P


def select_blocks(chosen, chosen_cols, wanted):
    hits = chosen_cols[..., :, None] == wanted
    total = None
    for slot_t in range(chosen.shape[-3]):
        term = jnp.where(
            hits[..., slot_t, :, None, None],
            chosen[..., slot_t, None, :, :],
            jnp.zeros((), chosen.dtype),
        )
        total = term if total is None else total + term
    return total


def term_maker(slab, slab_cols, local_b, local_bcols, pattern):
    total_rows = slab.shape[0]
    slots = slab.shape[2]
    width = slab.shape[3]
    slab = slab.reshape(total_rows, slots, width, width)
    slab_cols = slab_cols.reshape(total_rows, slots)

    def partial_term(start, count):
        group = math.gcd(count, 2)

        def one_group(index):
            first = index * group
            left = lax.dynamic_slice_in_dim(slab, first, group, 0)
            where_k = lax.dynamic_slice_in_dim(slab_cols, first, group, 0)
            wanted = lax.dynamic_slice_in_dim(pattern, first, group, 0)
            chosen = jnp.take(local_b, where_k, axis=0)
            chosen_cols = jnp.take(local_bcols, where_k, axis=0)
            picked = select_blocks(chosen, chosen_cols, wanted[:, None, None, :])
            return jnp.einsum("isab,iscbd->icad", left, picked, preferred_element_type=jnp.float32)

        terms = lax.map(one_group, jnp.arange(count // group, dtype=jnp.int32))
        return terms.reshape(count, pattern.shape[1], width, width)

    return partial_term


def per_device(a_blocks, a_cols, b_blocks, b_cols, c_cols):
    own_rows = a_blocks.shape[0]
    local_b = b_blocks[:, 0]
    local_bcols = b_cols[:, 0]
    pattern = c_cols[:, 0]
    per_pattern = pattern.shape[1]
    whole = lax.all_gather(a_blocks, "rep", axis=4, tiled=True)
    slab, slab_cols = (
        lax.all_to_all(whole, "blk", split_axis=1, concat_axis=0, tiled=True),
        lax.all_to_all(a_cols, "blk", split_axis=1, concat_axis=0, tiled=True),
    )
    partial_term = term_maker(slab, slab_cols, local_b, local_bcols, pattern)
    mine = lax.psum_scatter(
        partial_term(jnp.int32(0), own_rows * lax.axis_size("blk")),
        "blk",
        scatter_dimension=0,
        tiled=True,
    )
    width = a_blocks.shape[3]
    return mine.reshape(own_rows, 1, per_pattern, width, width)


def solution(mesh):
    placed = (
        P("blk", None, None, None, "rep"),
        P("blk", None, None),
        P("blk", "rep", None, None, None),
        P("blk", "rep", None),
        P(None, "rep", None),
    )
    return jax.shard_map(
        per_device,
        mesh=mesh,
        in_specs=placed,
        out_specs=P("blk", "rep", None, None, None),
        check_vma=False,
    )
```

profile of v0, /device:TPU:26, one launch (start us, length us, event | category | flops | bytes accessed | tf_op | source)
XLA Modules:
  0.0 730.4 jit_solution(5404238477490479959)
XLA Ops:
  6.5 1.9 copy.33
  8.6 16.9 %all_to_all.30 = s32[3,16,6]{2,0,1:T(4,128)S(1)} all-to-all(s32[3,16,6]{2,0,1:T(4,128)S(1)} %copy.29), channel_id=1, replica_groups=mesh['blk'=16,'rep'=16] {'blk'}, dimensions={1} | all-to-all | bytes 2304 | tf_op jit(solution)/shard_map/all_to_all | solution.py:57
  25.5 71.7 %all-gather.2.cloned.1.call-done = bf16[3,16,6,128,128]{3,4,2,0,1:T(8,128)(2,1)} async-done(((bf16[3,16,6,128,8]{3,4,2,0,1:T(8,128)(2,1)}), bf16[3,16,6,128,128]{3,4,2,0,1:T(8,128)(2,1)}) %all-gather.2.cloned.1.call-update) | async-done | bytes 9437200 | tf_op jit(solution)/shard_map/all_gather | solution.py:54
  97.2 8.5 %all-to-all-start.1 = ((bf16[3,16,6,128,128]{3,4,2,0,1:T(8,128)(2,1)}), bf16[3,16,6,128,128]{3,4,2,0,1:T(8,128)(2,1)}, u32[]{:S(2)}, u32[]{:S(2)}) async-start(bf16[3,16,6,128,128]{3,4,2,0,1:T(8,128)(2,1)} %all-gather.2.cloned.1.call-done), calls=%async_computation.1 | async-start | bytes 18874368 | tf_op jit(solution)/shard_map/all_to_all | solution.py:56
  106.0 210.0 %all-to-all-done.1 = bf16[3,16,6,128,128]{3,4,2,0,1:T(8,128)(2,1)} async-done(((bf16[3,16,6,128,128]{3,4,2,0,1:T(8,128)(2,1)}), bf16[3,16,6,128,128]{3,4,2,0,1:T(8,128)(2,1)}, u32[]{:S(2)}, u32[]{:S(2)}) %all-to-all-start.1) | async-done | bytes 9437216 | tf_op jit(solution)/shard_map/all_to_all | solution.py:56
  316.1 259.3 %while.10 = (s32[]{:T(128)}, f32[24,2,4,128,128]{4,3,2,1,0:T(8,128)}, s32[24]{0:T(128)S(1)}, s32[48,6]{1,0:T(8,128)S(1)}, s32[112,3]{1,0:T(8,128)S(1)}, /*index=...) while((s32[]{:T(128)}, ...), condition=%wide.region_1.2_spmd, body=%wide.region_0.1_spmd.sunk | while | flops 205849856 | bytes 13638623 | solution.py:42
  318.3 4.9 gather_fusion.1
  324.2 1.6 fusion.25
  329.1 4.9 gather_fusion.1
  335.0 1.6 fusion.25
  339.9 4.9 gather_fusion.1
  345.8 1.6 fusion.25
  350.7 4.9 gather_fusion.1
  356.6 1.6 fusion.25
  361.5 4.9 gather_fusion.1
  372.3 4.9 gather_fusion.1
  383.1 4.9 gather_fusion.1
  389.0 1.6 fusion.25
  393.9 4.9 gather_fusion.1
  399.8 1.6 fusion.25
  404.7 4.9 gather_fusion.1
  410.6 1.6 fusion.25
  415.5 4.9 gather_fusion.1
  421.4 1.6 fusion.25
  426.3 4.9 gather_fusion.1
  432.2 1.6 fusion.25
  437.2 4.9 gather_fusion.1
  443.0 1.6 fusion.25
  448.0 4.9 gather_fusion.1
  453.8 1.6 fusion.25
  458.8 4.9 gather_fusion.1
  464.6 1.6 fusion.25
  469.5 4.9 gather_fusion.1
  475.4 1.6 fusion.25
  480.3 4.9 gather_fusion.1
  491.2 4.9 gather_fusion.1
  497.1 1.6 fusion.25
  502.0 4.9 gather_fusion.1
  507.9 1.6 fusion.25
  512.8 4.9 gather_fusion.1
  518.7 1.6 fusion.25
  523.6 4.9 gather_fusion.1
  534.4 4.9 gather_fusion.1
  545.2 4.9 gather_fusion.1
  551.1 1.6 fusion.25
  556.0 4.9 gather_fusion.1
  566.8 4.9 gather_fusion.1
  575.4 148.2 %reduce-scatter.2.cloned.1.call-done = f32[3,4,128,128]{3,2,1,0:T(8,128)} async-done(((f32[48,4,128,128]{3,2,1,0:T(8,128)}), f32[3,4,128,128]{3,2,1,0:T(8,128)}) %reduce-scatter.2.cloned.1.call-update) | async-done | bytes 786448 | tf_op jit(solution)/shard_map/reduce_scatter | solution.py:60
  (455 shorter events, 97.6 us)
Async XLA Ops:
  6.5 2.0 copy-start
  6.5 90.7 %all-gather.2.cloned.1.call-start = ((), (), s32[]{:S(2)}) async-start(), calls=%async_computation.3 | async-start | bytes 10027008 | tf_op jit(solution)/shard_map/all_gather | solution.py:54
  25.5 80.3 %copy-start.2 = (s32[112,1,3]{0,1,2:T(1,128)S(1)}, s32[112,1,3]{0,1,2:T(1,128)}, u32[]{:S(2)}) copy-start(s32[112,1,3]{0,1,2:T(1,128)} %param.10) | copy-start | bytes 4036
  25.5 80.4 %copy-start.1 = (s32[48,1,4]{0,2,1:T(4,128)S(1)}, s32[48,1,4]{0,2,1:T(4,128)}, u32[]{:S(2)}) copy-start(s32[48,1,4]{0,2,1:T(4,128)} %param.11) | copy-start | bytes 2308
  97.2 218.8 %all-to-all-start.1 = ((bf16[3,16,6,128,128]{3,4,2,0,1:T(8,128)(2,1)}), bf16[3,16,6,128,128]{3,4,2,0,1:T(8,128)(2,1)}, u32[]{:S(2)}, u32[]{:S(2)}) async-start(bf16[3,16,6,128,128]{3,4,2,0,1:T(8,128)(2,1)} %all-gather.2.cloned.1.call-done), calls=%async_computation.1 | async-start | bytes 18874368 | tf_op jit(solution)/shard_map/all_to_all | solution.py:56
  105.7 617.8 %reduce-scatter.2.cloned.1.call-start = ((), (), s32[]{:S(2)}) async-start(), calls=%async_computation.4 | async-start | bytes 13369344 | tf_op jit(solution)/shard_map/reduce_scatter | solution.py:60
Sparse Core Ops, SparseCore 0:
  10.0 87.2 all-gather.1
  575.5 147.9 reduce-scatter.1
where the time goes:
time: 735 us; the launch traced here: 730 us
  waiting for transfers between devices  430 us (59%)
  local copies, waits for them, and re-layouts  199 us (27%)
  matrix products  39.1 us (5%)
  blocking collectives  16.9 us (2%)
  loops' own time  16.8 us (2%)
  between operations  13.4 us (2%)
  starting transfers between devices  8.53 us (1%)
    all_to_all x1, waiting for transfers between devices, per_device(): lax.all_to_all(whole, 'blk', split_axis=1, concat_axis=0, tiled=True)  210 us
    reduce_scatter x1, waiting for transfers between devices, per_device(): lax.psum_scatter(partial_term(jnp.int32(0), own_rows * lax.axis_size('blk...  148 us
    gather x24, local copies, waits for them, and re-layouts, one_group(): chosen = jnp.take(local_b, where_k, axis=0)  118 us
    all_gather x1, waiting for transfers between devices, per_device(): whole = lax.all_gather(a_blocks, 'rep', axis=4, tiled=True)  71.7 us
    dot_general x24, matrix products, one_group(): jnp.einsum('isab,iscbd->icad', left, picked, preferred_element_type=jnp.f...  39.1 us
    dynamic_update_slice x48, local copies, waits for them, and re-layouts, partial_term(): terms = lax.map(one_group, jnp.arange(count // group, dtype=jnp.int32))  25.2 us
    broadcast_in_dim x120, local copies, waits for them, and re-layouts, select_blocks(): jnp.where(hits[..., slot_t, :, None, None], chosen[..., slot_t, None, :,...  18.6 us
    gather x72, local copies, waits for them, and re-layouts, one_group(): chosen_cols = jnp.take(local_bcols, where_k, axis=0)  17.6 us
  transfers between devices with their start and end apart: 3, of which 3 were waited for; matrix products, arithmetic and copies ran while one was open for 0% of the time, Pallas kernels for 0%

commit v1 on v0

v1 whole, which is shorter than its diff:
```python
import jax
import jax.numpy as jnp
from jax import lax
from jax.experimental import pallas as pl
from jax.experimental.pallas import tpu as pltpu
from jax.sharding import PartitionSpec as P

MESH = pl.DeviceIdType.MESH
NX, NZ = 2, 8
NY, NXH, NC = 4, 2, 2
NREP = NY * NXH * NC
ROWS, KA, KB, KC, BS, KP = 3, 6, 3, 4, 128, 112
HALF = BS // 2
PIECE = KA * BS // NREP
BLOCKS = ROWS * 2
ZERO = KP * KB
Z_SENDS, X_SENDS = 21, 9
Z_RECVS, X_RECVS = 24, 9
DUMMY = Z_RECVS + X_RECVS
FAR, NEAR, DONE = 0, 1, 2
FIRST_COL = (0, 0, 2)


def step_of(e):
    far = (8 - e) // 2
    return far * (2 * (e % 2) - 1) + NZ


def kernel(
    a_ref, cols_ref, b_hbm, table_hbm, out_ref,
    g, b, picked, part, cols_v, cols_s, table_s, sd, ss, rd, rs,
    ga_send, ga_recv, gc_send, gc_recv, cols_sem, load_sem,
    rep_send, rep_recv, d_send, s_send, d_recv, s_recv,
):
    q, t = lax.axis_index("blk"), lax.axis_index("rep")
    xl, z = q // NZ, q % NZ
    y, xh, core = t // (NXH * NC), (t // NC) % NXH, t % NC

    def blk_at(x, zz):
        return (x * NZ + zz % NZ, t)

    def slot(yy, h, c):
        return (yy % NY) * (NXH * NC) + h * NC + c

    def rep_at(yy, h, c):
        return (q, slot(yy, h, c))

    load_b = pltpu.make_async_copy(b_hbm, b.at[pl.ds(0, ZERO)], load_sem.at[0])
    load_t = pltpu.make_async_copy(table_hbm, table_s, load_sem.at[1])
    load_b.start()
    load_t.start()
    own_a = pltpu.make_async_copy(a_ref.at[:, q], g.at[t, 7, 0], load_sem.at[2])
    own_c = pltpu.make_async_copy(cols_ref.at[q], cols_v.at[7, 0], load_sem.at[3])
    own_a.start()
    own_c.start()

    barrier = pltpu.get_barrier_semaphore()

    def greet(n, carry):
        pl.semaphore_signal(barrier, inc=1, device_id=((q + n) % (NX * NZ), t), device_id_type=MESH)
        return carry

    lax.fori_loop(1, NX * NZ, greet, 0)
    for peer in (rep_at(y, 1 - xh, core), rep_at(y, xh, 1 - core), rep_at(y + 1, xh, core), rep_at(y + 2, xh, core), rep_at(y + 3, xh, core)):
        pl.semaphore_signal(barrier, inc=1, device_id=peer, device_id_type=MESH)
    pl.semaphore_wait(barrier, NX * NZ - 1 + 5)

    def over_blk(n):
        e, rel = n // 2, n % 2 + n // 14
        x, zz = (xl + rel) % NX, (z + 2 * NZ - step_of(e)) % NZ
        to = x * NZ + zz
        return (
            pltpu.make_async_remote_copy(
                a_ref.at[:, to], g.at[t, e, rel], ga_send.at[e, rel], ga_recv.at[e, rel], device_id=(to, t), device_id_type=MESH
            ),
            pltpu.make_async_remote_copy(
                cols_ref.at[to], cols_v.at[e, rel], gc_send.at[e, rel], gc_recv.at[e, rel], device_id=(to, t), device_id_type=MESH
            ),
        )

    def send_blk(n, carry):
        for copy in over_blk(n):
            copy.start()
        return carry

    lax.fori_loop(0, 15, send_blk, 0)

    b[ZERO] = jnp.zeros((BS, BS), b.dtype)
    rd[DUMMY] = jnp.zeros(rd.shape[1:], rd.dtype)
    rs[DUMMY] = jnp.zeros(rs.shape[1:], rs.dtype)

    def over_rep(e, piece, n, to):
        return pltpu.make_async_remote_copy(
            g.at[piece, e], g.at[piece, e], rep_send.at[e, n], rep_recv.at[e, piece], device_id=to, device_id_type=MESH
        )

    def arrived(e, piece):
        over_rep(e, piece, 0, rep_at(y, xh, 1 - core)).wait_recv()

    def first_sends(e):
        own = slot(y, xh, core)
        yield over_rep(e, own, 0, rep_at(y, 1 - xh, core))
        yield over_rep(e, own, 1, rep_at(y + 1, xh, core))
        yield over_rep(e, own, 2, rep_at(y + 3, xh, core))
        yield over_rep(e, own, 3, rep_at(y + 2, xh, core))
        yield over_rep(e, own, 4, rep_at(y, xh, 1 - core))

    def second_sends(e):
        other = slot(y, 1 - xh, core)
        yield over_rep(e, other, 5, rep_at(y + 1, xh, core))
        yield over_rep(e, other, 6, rep_at(y + 3, xh, core))
        yield over_rep(e, other, 7, rep_at(y + 2, xh, core))
        yield over_rep(e, other, 8, rep_at(y, xh, 1 - core))

    def third_sends(e):
        n = 9
        for d in (1, 3, 2):
            for h in (0, 1):
                piece = slot(y + d, (xh + h) % NXH, core)
                arrived(e, piece)
                yield over_rep(e, piece, n, rep_at(y, xh, 1 - core))
                n += 1

    def stage_a(e):
        for rel in (1, 0):
            def remote():
                copies = over_blk(2 * e + rel - e // 7)
                for copy in copies:
                    copy.wait_recv()

            if rel:
                remote()
            else:
                pl.when(e < 7)(remote)

                @pl.when(e == 7)
                def _():
                    own_a.wait()
                    own_c.wait()

        pltpu.make_async_copy(cols_v.at[e], cols_s.at[e], cols_sem.at[e]).start()
        for copy in first_sends(e):
            copy.start()

    def stage_b(e):
        arrived(e, slot(y, 1 - xh, core))
        for copy in second_sends(e):
            copy.start()

    def stage_c(e):
        for copy in third_sends(e):
            copy.start()

    def multiply(e):
        for yy in range(NY):
            for h in range(NXH):
                arrived(e, slot(yy, h, 1 - core))
        pltpu.make_async_copy(cols_v.at[e], cols_s.at[e], cols_sem.at[e]).wait()

        def one_row(n, carry):
            rel, r = n // ROWS, n % ROWS
            owner = ((xl + rel) % NX) * NZ + (z + step_of(e)) % NZ
            row = (owner * ROWS + r) * KC
            for s in range(KA):
                k = cols_s[e, rel, 0, r * KA + s]
                for c in range(KC):
                    which = table_s[row + c, k]
                    picked[pl.ds(s * BS, BS), pl.ds(c * BS, BS)] = b[which]
            left = g[:, e, rel, r].astype(jnp.float32).reshape(NREP, KA, BS // NREP, BS)
            left = jnp.concatenate([left[:, s].reshape(BS, BS) for s in range(KA)], axis=0).astype(b.dtype)
            total = lax.dot_general(left, picked[...], (((0,), (0,)), ((), ())), preferred_element_type=jnp.float32)
            for c in range(KC):
                part[rel, r, c] = total[:, c * BS : (c + 1) * BS]
            return carry

        lax.fori_loop(0, 2 * ROWS, one_row, 0)

    def message(frm, to_slot, to):
        return (
            pltpu.make_async_remote_copy(sd.at[frm], rd.at[to_slot], d_send.at[frm], d_recv.at[to_slot], device_id=to, device_id_type=MESH),
            pltpu.make_async_remote_copy(ss.at[frm], rs.at[to_slot], s_send.at[frm], s_recv.at[to_slot], device_id=to, device_id_type=MESH),
        )

    def received(at):
        for copy in message(0, at, blk_at(1 - xl, z)):
            copy.wait_recv()

    def totals(rel, first_col, at, j):
        r, c = j // 2, first_col + j % 2
        low, high = part[rel, r, c, pl.ds(0, HALF)], part[rel, r, c, pl.ds(HALF, HALF)]
        for n in at:
            word, scale = rd[n, j], rs[n, pl.ds(j, 1)]
            low += ((word & 0xFFFF).astype(jnp.float32) - 32768.0) * scale
            high += (lax.shift_right_logical(word, 16).astype(jnp.float32) - 32768.0) * scale
        return low, high

    def pack(rel, first_col, at, to_slot):
        def one(j, carry):
            low, high = totals(rel, first_col, at, j)
            top = jnp.maximum(jnp.max(jnp.maximum(jnp.abs(low), jnp.abs(high)), axis=0, keepdims=True), 1e-33)
            gain = 32767.0 / top
            low = (low * gain + 32768.5).astype(jnp.int32)
            high = (high * gain + 32768.5).astype(jnp.int32)
            sd[to_slot, j] = low | (high << 16)
            ss[to_slot, pl.ds(j, 1)] = top * (1.0 / 32767.0)
            return carry

        lax.fori_loop(0, BLOCKS, one, 0)

    def keep(first_col, at):
        def one(j, carry):
            low, high = totals(0, first_col, at, j)
            r, c = j // 2, first_col + j % 2
            out_ref[r, c, pl.ds(0, HALF)] = low
            out_ref[r, c, pl.ds(HALF, HALF)] = high
            return carry

        lax.fori_loop(0, BLOCKS, one, 0)

    def z_slot(e, kind):
        return (e - 1) * 3 + kind

    def along_z(e, kind):
        up = jnp.where(e == 0, jnp.int32(kind != NEAR), e % 2)
        at = jnp.where(e == 0, 2 - up, e + 2)
        return message(e * 3 + kind, z_slot(at, kind), blk_at(xl, z + NZ + 2 * up - 1))

    def has_z(e, kind):
        return (e >= 3) | (e == (2 if kind == NEAR else 1))

    def pass_on(e, kind):
        at = [jnp.where(has_z(e, kind), z_slot(e, kind), DUMMY)]
        if kind == DONE:
            received(Z_RECVS + e)
            at.append(Z_RECVS + e)

        @pl.when(has_z(e, kind))
        def _():
            received(z_slot(e, kind))

        pack(int(kind == FAR), FIRST_COL[kind], at, e * 3 + kind)
        for copy in along_z(e, kind):
            copy.start()

    def across_x(n):
        return message(Z_SENDS + n, Z_RECVS + n, blk_at(1 - xl, z))

    def send_x(n, at, first_col):
        pack(1, first_col, at, Z_SENDS + n)
        for copy in across_x(n):
            copy.start()

    load_b.wait()
    load_t.wait()

    def one_step(i, carry):
        pl.when(i < 8)(lambda: stage_a(i))
        pl.when((i >= 1) & (i < 9))(lambda: stage_b(i - 1))

        @pl.when(i >= 2)
        def _():
            e = i - 2
            stage_c(e)
            pl.when(e >= 1)(lambda: pass_on(e - 1, DONE))
            multiply(e)
            send_x(e, [], FIRST_COL[DONE])

            @pl.when(e < 7)
            def _():
                pass_on(e, FAR)
                pass_on(e, NEAR)

        return carry

    lax.fori_loop(0, 10, one_step, 0)

    for kind in (FAR, DONE, NEAR):
        for e in (7, 8):
            received(z_slot(e, kind))
        at = [z_slot(7, kind), z_slot(8, kind)]
        if kind == FAR:
            send_x(8, at, FIRST_COL[kind])
        else:
            last = Z_RECVS + (7 if kind == DONE else 8)
            received(last)
            keep(FIRST_COL[kind], at + [last])

    def sent_blk(n, carry):
        for copy in over_blk(n):
            copy.wait_send()
        return carry

    lax.fori_loop(0, 15, sent_blk, 0)

    def sent_rep(e, carry):
        for n in range(9 + 6):
            over_rep(e, t, n, rep_at(y, xh, 1 - core)).wait_send()
        return carry

    lax.fori_loop(0, 8, sent_rep, 0)

    def sent_messages(n, carry):
        for copy in message(n, 0, blk_at(1 - xl, z)):
            copy.wait_send()
        return carry

    lax.fori_loop(0, Z_SENDS + X_SENDS, sent_messages, 0)


def per_device(a_blocks, a_cols, b_blocks, b_cols, c_cols):
    panels = a_blocks.shape[1]
    pieces = jnp.swapaxes(a_blocks, 3, 4).reshape(ROWS, panels, PIECE, BS)
    lists = jnp.swapaxes(a_cols, 0, 1).reshape(panels, 1, ROWS * KA)
    lists = jnp.pad(lists, ((0, 0), (0, 7), (0, 128 - ROWS * KA)))
    wanted = c_cols[:, 0].reshape(-1, 1)
    have = b_cols[:, 0]
    table = jnp.full((wanted.shape[0], KP), ZERO, jnp.int32)
    for slot_t in range(KB):
        table = jnp.where(have[:, slot_t][None, :] == wanted, jnp.arange(KP, dtype=jnp.int32) * KB + slot_t, table)
    table = jnp.pad(table, ((0, 0), (0, 128 - KP)))
    any_ref = pl.BlockSpec(memory_space=pl.ANY)
    vmem = pltpu.VMEM
    dma = pltpu.SemaphoreType.DMA
    mine = pl.pallas_call(
        kernel,
        out_shape=jax.ShapeDtypeStruct((ROWS, KC, BS, BS), jnp.float32),
        in_specs=[any_ref] * 4,
        out_specs=pl.BlockSpec(memory_space=pltpu.VMEM),
        scratch_shapes=[
            vmem((NREP, 8, 2, ROWS, PIECE, BS), jnp.bfloat16),
            vmem((ZERO + 1, BS, BS), jnp.bfloat16),
            vmem((KA * BS, KC * BS), jnp.bfloat16),
            vmem((2, ROWS, KC, BS, BS), jnp.float32),
            vmem((8, 2, 8, 128), jnp.int32),
            pltpu.SMEM((8, 2, 8, 128), jnp.int32),
            pltpu.SMEM((table.shape[0], 128), jnp.int32),
            vmem((Z_SENDS + X_SENDS, BLOCKS, HALF, BS), jnp.int32),
            vmem((Z_SENDS + X_SENDS, 8, BS), jnp.float32),
            vmem((DUMMY + 1, BLOCKS, HALF, BS), jnp.int32),
            vmem((DUMMY + 1, 8, BS), jnp.float32),
            dma((8, 2)), dma((8, 2)), dma((8, 2)), dma((8, 2)), dma((8,)), dma((4,)),
            dma((8, 15)), dma((8, NREP)),
            dma((Z_SENDS + X_SENDS,)), dma((Z_SENDS + X_SENDS,)), dma((DUMMY,)), dma((DUMMY,)),
        ],
        compiler_params=pltpu.CompilerParams(collective_id=0, has_side_effects=True, vmem_limit_bytes=56 * 2**20),
        name="block_product",
    )(pieces, lists, b_blocks.reshape(KP * KB, BS, BS), table)
    return mine.reshape(ROWS, 1, KC, BS, BS)


def solution(mesh):
    placed = (
        P("blk", None, None, None, "rep"),
        P("blk", None, None),
        P("blk", "rep", None, None, None),
        P("blk", "rep", None),
        P(None, "rep", None),
    )
    return jax.shard_map(
        per_device,
        mesh=mesh,
        in_specs=placed,
        out_specs=P("blk", "rep", None, None, None),
        check_vma=False,
    )
```

time: 735 us -> 121 us (0.16)
  waiting for transfers between devices: 430 us -> 0 us
  local copies, waits for them, and re-layouts: 199 us -> 5.69 us
  Pallas kernels: 0 us -> 115 us
  matrix products: 39.1 us -> 0 us
  blocking collectives: 16.9 us -> 0 us
  loops' own time: 16.8 us -> 0 us
  between operations: 13.4 us -> 0.02 us
  starting transfers between devices: 8.53 us -> 0 us
    all_to_all x1 -> x0, waiting for transfers between devices: 210 us -> none  [per_device(): lax.all_to_all(whole, 'blk', split_axis=1, concat_axis=0, tiled=True)]
    reduce_scatter x1 -> x0, waiting for transfers between devices: 148 us -> none  [per_device(): lax.psum_scatter(partial_term(jnp.int32(0), own_rows * lax.axis_size('blk...]
    gather x96 -> x0, local copies, waits for them, and re-layouts: 135 us -> none  [the longest x24 118 us: one_group(): chosen = jnp.take(local_b, where_k, axis=0)]
    pallas_call x0 -> x1, Pallas kernels: none -> 115 us  [per_device(): pl.pallas_call(kernel, out_shape=jax.ShapeDtypeStruct((ROWS, KC, BS, BS),...]
    all_gather x1 -> x0, waiting for transfers between devices: 71.7 us -> none  [per_device(): whole = lax.all_gather(a_blocks, 'rep', axis=4, tiled=True)]
    dot_general x24 -> x0, matrix products: 39.1 us -> none  [one_group(): jnp.einsum('isab,iscbd->icad', left, picked, preferred_element_type=jnp.f...]
    dynamic_update_slice x48 -> x0, local copies, waits for them, and re-layouts: 25.2 us -> none  [partial_term(): terms = lax.map(one_group, jnp.arange(count // group, dtype=jnp.int32))]
    broadcast_in_dim x144 -> x0, local copies, waits for them, and re-layouts: 20.6 us -> none  [the longest x120 18.6 us: select_blocks(): jnp.where(hits[..., slot_t, :, None, None], chosen[..., slot_t, None, :,...]
  transfers between devices with their start and end apart: 3 -> 0, of which waited for: 3 -> 0; matrix products, arithmetic and copies ran while one was open for 0% -> 0% of each run, Pallas kernels for 0% -> 0%
where the time goes in v1:
time: 121 us; the launch traced here: 120 us
  Pallas kernels  115 us (95%)
  local copies, waits for them, and re-layouts  5.69 us (5%)
    pallas_call x1, Pallas kernels, per_device(): pl.pallas_call(kernel, out_shape=jax.ShapeDtypeStruct((ROWS, KC, BS, BS),...  115 us
    unnamed x3, local copies, waits for them, and re-layouts  3.51 us

profile of v1, /device:TPU:26, one launch (start us, length us, event | category | flops | bytes accessed | tf_op | source)
XLA Modules:
  0.0 120.4 jit_solution(11378161150276658320)
XLA Ops:
  0.0 0.7 copy.13
  0.7 0.7 reshape.17
  1.4 0.1 copy.8
  1.5 0.8 copy.9
  2.3 0.1 eq.45
  2.4 0.6 pad.8.cols_ref
  3.0 0.1 select_select_fusion
  3.1 0.7 pad.9.table_hbm
  3.7 114.6 %block_product.1 = f32[3,4,128,128]{3,2,1,0:T(8,128)} custom-call(bf16[3,16,48,128]{3,2,1,0:T(8,128)(2,1)} %bitcast.23, s32[16,8,128]{2,1,0:T(8,128)} %pad.8.cols_ref, bf16[336,128,128]{2,1,0:T(8,128)(2,1)} %bitcast.21, s32[192,128]{1,0:T(8,128)} %pad.9.table_hbm), custom_call_target="tpu_custom_call" | custom-call | tf_op jit(solution)/shard_map/block_product/pallas_call | solution.py:324
  118.3 2.1 %copy.15 = f32[3,1,4,128,128]{4,3,2,1,0:T(8,128)} copy(f32[3,1,4,128,128]{4,3,2,1,0:T(8,128)} %bitcast.22) | data formatting | bytes 1572864
  (3 shorter events, 0.0 us)

commit v2 on v1

--- a/solution.py
+++ b/solution.py
@@ -19,6 +19,8 @@
 DUMMY = Z_RECVS + X_RECVS
 FAR, NEAR, DONE = 0, 1, 2
 FIRST_COL = (0, 0, 2)
+LEAD_A, LEAD_B, LEAD_C, LEAD_D = 4, 3, 2, 1
+AHEAD = 4
 
 
 def step_of(e):
@@ -39,17 +41,19 @@
     def blk_at(x, zz):
         return (x * NZ + zz % NZ, t)
 
+    def rep_at(yy, h, c):
+        return (q, (yy % NY) * (NXH * NC) + h * NC + c)
+
     def slot(yy, h, c):
-        return (yy % NY) * (NXH * NC) + h * NC + c
-
-    def rep_at(yy, h, c):
-        return (q, slot(yy, h, c))
+        return c * (NY * NXH) + (yy % NY) * NXH + h
+
+    me = slot(y, xh, core)
 
     load_b = pltpu.make_async_copy(b_hbm, b.at[pl.ds(0, ZERO)], load_sem.at[0])
     load_t = pltpu.make_async_copy(table_hbm, table_s, load_sem.at[1])
     load_b.start()
     load_t.start()
-    own_a = pltpu.make_async_copy(a_ref.at[:, q], g.at[t, 7, 0], load_sem.at[2])
+    own_a = pltpu.make_async_copy(a_ref.at[:, q], g.at[me, 7, 0], load_sem.at[2])
     own_c = pltpu.make_async_copy(cols_ref.at[q], cols_v.at[7, 0], load_sem.at[3])
     own_a.start()
     own_c.start()
@@ -61,9 +65,9 @@
         return carry
 
     lax.fori_loop(1, NX * NZ, greet, 0)
-    for peer in (rep_at(y, 1 - xh, core), rep_at(y, xh, 1 - core), rep_at(y + 1, xh, core), rep_at(y + 2, xh, core), rep_at(y + 3, xh, core)):
+    for peer in (rep_at(y, 1 - xh, core), rep_at(y, xh, 1 - core), rep_at(y + 1, xh, core), rep_at(y + 3, xh, core)):
         pl.semaphore_signal(barrier, inc=1, device_id=peer, device_id_type=MESH)
-    pl.semaphore_wait(barrier, NX * NZ - 1 + 5)
+    pl.semaphore_wait(barrier, NX * NZ - 1 + 4)
 
     def over_blk(n):
         e, rel = n // 2, n % 2 + n // 14
@@ -71,55 +75,65 @@
         to = x * NZ + zz
         return (
             pltpu.make_async_remote_copy(
-                a_ref.at[:, to], g.at[t, e, rel], ga_send.at[e, rel], ga_recv.at[e, rel], device_id=(to, t), device_id_type=MESH
+                a_ref.at[:, to], g.at[me, e, rel], ga_send.at[e, rel], ga_recv.at[e, rel], device_id=(to, t), device_id_type=MESH
             ),
             pltpu.make_async_remote_copy(
                 cols_ref.at[to], cols_v.at[e, rel], gc_send.at[e, rel], gc_recv.at[e, rel], device_id=(to, t), device_id_type=MESH
             ),
         )
 
-    def send_blk(n, carry):
-        for copy in over_blk(n):
-            copy.start()
-        return carry
-
-    lax.fori_loop(0, 15, send_blk, 0)
+    def send_blk(e):
+        for copy in over_blk(2 * e + 1 - e // 7):
+            copy.start()
+
+        @pl.when(e < 7)
+        def _():
+            for copy in over_blk(2 * e):
+                copy.start()
+
+    for e in range(AHEAD):
+        send_blk(jnp.int32(e))
 
     b[ZERO] = jnp.zeros((BS, BS), b.dtype)
     rd[DUMMY] = jnp.zeros(rd.shape[1:], rd.dtype)
     rs[DUMMY] = jnp.zeros(rs.shape[1:], rs.dtype)
 
-    def over_rep(e, piece, n, to):
+    def one_piece(e, piece, n, to):
         return pltpu.make_async_remote_copy(
             g.at[piece, e], g.at[piece, e], rep_send.at[e, n], rep_recv.at[e, piece], device_id=to, device_id_type=MESH
         )
 
-    def arrived(e, piece):
-        over_rep(e, piece, 0, rep_at(y, xh, 1 - core)).wait_recv()
+    def two_pieces(e, yy, c, n, to):
+        first = slot(yy, 0, c)
+        both = g.at[pl.ds(first, 2), e]
+        return pltpu.make_async_remote_copy(
+            both, both, rep_send.at[e, n], rep_recv.at[e, first], device_id=to, device_id_type=MESH
+        )
+
+    other_core = rep_at(y, xh, 1 - core)
+    above, below = rep_at(y + 1, xh, core), rep_at(y + 3, xh, core)
 
     def first_sends(e):
-        own = slot(y, xh, core)
-        yield over_rep(e, own, 0, rep_at(y, 1 - xh, core))
-        yield over_rep(e, own, 1, rep_at(y + 1, xh, core))
-        yield over_rep(e, own, 2, rep_at(y + 3, xh, core))
-        yield over_rep(e, own, 3, rep_at(y + 2, xh, core))
-        yield over_rep(e, own, 4, rep_at(y, xh, 1 - core))
+        yield one_piece(e, me, 0, rep_at(y, 1 - xh, core))
 
     def second_sends(e):
-        other = slot(y, 1 - xh, core)
-        yield over_rep(e, other, 5, rep_at(y + 1, xh, core))
-        yield over_rep(e, other, 6, rep_at(y + 3, xh, core))
-        yield over_rep(e, other, 7, rep_at(y + 2, xh, core))
-        yield over_rep(e, other, 8, rep_at(y, xh, 1 - core))
+        one_piece(e, slot(y, 1 - xh, core), 0, other_core).wait_recv()
+        yield two_pieces(e, y, core, 1, above)
+        yield two_pieces(e, y, core, 2, below)
+        yield two_pieces(e, y, core, 3, other_core)
 
     def third_sends(e):
-        n = 9
-        for d in (1, 3, 2):
-            for h in (0, 1):
-                piece = slot(y + d, (xh + h) % NXH, core)
-                arrived(e, piece)
-                yield over_rep(e, piece, n, rep_at(y, xh, 1 - core))
-                n += 1
+        two_pieces(e, y + 3, core, 0, other_core).wait_recv()
+        yield one_piece(e, slot(y + 3, 0, core), 4, above)
+        yield two_pieces(e, y + 3, core, 5, other_core)
+        two_pieces(e, y + 1, core, 0, other_core).wait_recv()
+        yield one_piece(e, slot(y + 1, 1, core), 6, below)
+        yield two_pieces(e, y + 1, core, 7, other_core)
+
+    def fourth_sends(e):
+        for h in (0, 1):
+            one_piece(e, slot(y + 2, h, core), 0, other_core).wait_recv()
+        yield two_pieces(e, y + 2, core, 8, other_core)
 
     def stage_a(e):
         for rel in (1, 0):
@@ -143,7 +157,6 @@
             copy.start()
 
     def stage_b(e):
-        arrived(e, slot(y, 1 - xh, core))
         for copy in second_sends(e):
             copy.start()
 
@@ -151,29 +164,34 @@
         for copy in third_sends(e):
             copy.start()
 
+    def stage_d(e):
+        for copy in fourth_sends(e):
+            copy.start()
+
     def multiply(e):
         for yy in range(NY):
-            for h in range(NXH):
-                arrived(e, slot(yy, h, 1 - core))
+            two_pieces(e, yy, 1 - core, 0, other_core).wait_recv()
         pltpu.make_async_copy(cols_v.at[e], cols_s.at[e], cols_sem.at[e]).wait()
 
-        def one_row(n, carry):
-            rel, r = n // ROWS, n % ROWS
+        def one_rel(rel, carry):
             owner = ((xl + rel) % NX) * NZ + (z + step_of(e)) % NZ
-            row = (owner * ROWS + r) * KC
-            for s in range(KA):
-                k = cols_s[e, rel, 0, r * KA + s]
+            for r in range(ROWS):
+                row = (owner * ROWS + r) * KC
+                for s in range(KA):
+                    k = cols_s[e, rel, r, s]
+                    for c in range(KC):
+                        which = table_s[row + c, k]
+                        picked[r, pl.ds(s * BS, BS), pl.ds(c * BS, BS)] = b[which]
+            for r in range(ROWS):
+                left = g[:, e, rel, r].astype(jnp.float32).reshape(NC, NY * NXH, KA, BS // NREP, BS)
+                left = [left[c, m, s] for s in range(KA) for m in range(NY * NXH) for c in range(NC)]
+                left = jnp.concatenate(left, axis=0).astype(b.dtype)
+                total = lax.dot_general(left, picked[r], (((0,), (0,)), ((), ())), preferred_element_type=jnp.float32)
                 for c in range(KC):
-                    which = table_s[row + c, k]
-                    picked[pl.ds(s * BS, BS), pl.ds(c * BS, BS)] = b[which]
-            left = g[:, e, rel, r].astype(jnp.float32).reshape(NREP, KA, BS // NREP, BS)
-            left = jnp.concatenate([left[:, s].reshape(BS, BS) for s in range(KA)], axis=0).astype(b.dtype)
-            total = lax.dot_general(left, picked[...], (((0,), (0,)), ((), ())), preferred_element_type=jnp.float32)
-            for c in range(KC):
-                part[rel, r, c] = total[:, c * BS : (c + 1) * BS]
+                    part[rel, r, c] = total[:, c * BS : (c + 1) * BS]
             return carry
 
-        lax.fori_loop(0, 2 * ROWS, one_row, 0)
+        lax.fori_loop(0, 2, one_rel, 0)
 
     def message(frm, to_slot, to):
         return (
@@ -250,18 +268,23 @@
         for copy in across_x(n):
             copy.start()
 
-    load_b.wait()
-    load_t.wait()
-
     def one_step(i, carry):
         pl.when(i < 8)(lambda: stage_a(i))
-        pl.when((i >= 1) & (i < 9))(lambda: stage_b(i - 1))
-
-        @pl.when(i >= 2)
+        pl.when(i + AHEAD < 8)(lambda: send_blk(i + AHEAD))
+        for lead, stage in ((LEAD_B, stage_b), (LEAD_C, stage_c), (LEAD_D, stage_d)):
+            n = i - LEAD_A + lead
+            pl.when((n >= 0) & (n < 8))(lambda stage=stage, n=n: stage(n))
+
+        @pl.when(i >= LEAD_A)
         def _():
-            e = i - 2
-            stage_c(e)
+            e = i - LEAD_A
             pl.when(e >= 1)(lambda: pass_on(e - 1, DONE))
+
+            @pl.when(e == 0)
+            def _():
+                load_b.wait()
+                load_t.wait()
+
             multiply(e)
             send_x(e, [], FIRST_COL[DONE])
 
@@ -272,52 +295,53 @@
 
         return carry
 
-    lax.fori_loop(0, 10, one_step, 0)
-
-    for kind in (FAR, DONE, NEAR):
+    lax.fori_loop(0, 8 + LEAD_A, one_step, 0)
+
+    def last_z(kind):
         for e in (7, 8):
             received(z_slot(e, kind))
-        at = [z_slot(7, kind), z_slot(8, kind)]
-        if kind == FAR:
-            send_x(8, at, FIRST_COL[kind])
-        else:
-            last = Z_RECVS + (7 if kind == DONE else 8)
-            received(last)
-            keep(FIRST_COL[kind], at + [last])
+        return [z_slot(7, kind), z_slot(8, kind)]
+
+    send_x(8, last_z(FAR), FIRST_COL[FAR])
 
     def sent_blk(n, carry):
         for copy in over_blk(n):
             copy.wait_send()
         return carry
 
-    lax.fori_loop(0, 15, sent_blk, 0)
-
     def sent_rep(e, carry):
-        for n in range(9 + 6):
-            over_rep(e, t, n, rep_at(y, xh, 1 - core)).wait_send()
-        return carry
-
-    lax.fori_loop(0, 8, sent_rep, 0)
+        for n in (0, 4, 6):
+            one_piece(e, me, n, other_core).wait_send()
+        for n in (1, 2, 3, 5, 7, 8):
+            two_pieces(e, y, core, n, other_core).wait_send()
+        return carry
 
     def sent_messages(n, carry):
         for copy in message(n, 0, blk_at(1 - xl, z)):
             copy.wait_send()
         return carry
 
-    lax.fori_loop(0, Z_SENDS + X_SENDS, sent_messages, 0)
+    lax.fori_loop(0, 15, sent_blk, 0)
+    lax.fori_loop(0, 8, sent_rep, 0)
+    received(Z_RECVS + 7)
+    keep(FIRST_COL[DONE], last_z(DONE) + [Z_RECVS + 7])
+    lax.fori_loop(0, Z_SENDS + X_SENDS - 1, sent_messages, 0)
+    near = last_z(NEAR)
+    received(Z_RECVS + 8)
+    keep(FIRST_COL[NEAR], near + [Z_RECVS + 8])
+    sent_messages(Z_SENDS + X_SENDS - 1, 0)
 
 
 def per_device(a_blocks, a_cols, b_blocks, b_cols, c_cols):
     panels = a_blocks.shape[1]
     pieces = jnp.swapaxes(a_blocks, 3, 4).reshape(ROWS, panels, PIECE, BS)
-    lists = jnp.swapaxes(a_cols, 0, 1).reshape(panels, 1, ROWS * KA)
-    lists = jnp.pad(lists, ((0, 0), (0, 7), (0, 128 - ROWS * KA)))
+    lists = jnp.pad(jnp.swapaxes(a_cols, 0, 1), ((0, 0), (0, 8 - ROWS), (0, 128 - KA)))
     wanted = c_cols[:, 0].reshape(-1, 1)
-    have = b_cols[:, 0]
-    table = jnp.full((wanted.shape[0], KP), ZERO, jnp.int32)
+    have = jnp.pad(jnp.swapaxes(b_cols[:, 0], 0, 1), ((0, 0), (0, 128 - KP)), constant_values=-1)
+    first = lax.broadcasted_iota(jnp.int32, (1, 128), 1) * KB
+    table = jnp.full((wanted.shape[0], 128), ZERO, jnp.int32)
     for slot_t in range(KB):
-        table = jnp.where(have[:, slot_t][None, :] == wanted, jnp.arange(KP, dtype=jnp.int32) * KB + slot_t, table)
-    table = jnp.pad(table, ((0, 0), (0, 128 - KP)))
+        table = jnp.where(have[slot_t : slot_t + 1] == wanted, first + slot_t, table)
     any_ref = pl.BlockSpec(memory_space=pl.ANY)
     vmem = pltpu.VMEM
     dma = pltpu.SemaphoreType.DMA
@@ -329,7 +353,7 @@
         scratch_shapes=[
             vmem((NREP, 8, 2, ROWS, PIECE, BS), jnp.bfloat16),
             vmem((ZERO + 1, BS, BS), jnp.bfloat16),
-            vmem((KA * BS, KC * BS), jnp.bfloat16),
+            vmem((ROWS, KA * BS, KC * BS), jnp.bfloat16),
             vmem((2, ROWS, KC, BS, BS), jnp.float32),
             vmem((8, 2, 8, 128), jnp.int32),
             pltpu.SMEM((8, 2, 8, 128), jnp.int32),
@@ -339,7 +363,7 @@
             vmem((DUMMY + 1, BLOCKS, HALF, BS), jnp.int32),
             vmem((DUMMY + 1, 8, BS), jnp.float32),
             dma((8, 2)), dma((8, 2)), dma((8, 2)), dma((8, 2)), dma((8,)), dma((4,)),
-            dma((8, 15)), dma((8, NREP)),
+            dma((8, 9)), dma((8, NREP)),
             dma((Z_SENDS + X_SENDS,)), dma((Z_SENDS + X_SENDS,)), dma((DUMMY,)), dma((DUMMY,)),
         ],
         compiler_params=pltpu.CompilerParams(collective_id=0, has_side_effects=True, vmem_limit_bytes=56 * 2**20),

time: 121 us -> 118 us (0.975)
  Pallas kernels: 115 us -> 111 us
    pallas_call x1, Pallas kernels: 115 us -> 111 us  [per_device(): pl.pallas_call(kernel, out_shape=jax.ShapeDtypeStruct((ROWS, KC, BS, BS),...]
    unnamed x3 -> x4, local copies, waits for them, and re-layouts: 3.51 us -> 4.32 us
where the time goes in v2:
time: 118 us; the launch traced here: 117 us
  Pallas kernels  111 us (94%)
  local copies, waits for them, and re-layouts  5.06 us (4%)
    pallas_call x1, Pallas kernels, per_device(): pl.pallas_call(kernel, out_shape=jax.ShapeDtypeStruct((ROWS, KC, BS, BS),...  111 us
    unnamed x4, local copies, waits for them, and re-layouts  4.32 us

profile of v2, /device:TPU:26, one launch (start us, length us, event | category | flops | bytes accessed | tf_op | source)
XLA Modules:
  0.0 116.7 jit_solution(12415985028195261626)
XLA Ops:
  0.0 0.7 copy.13
  0.7 0.8 copy.9
  1.5 0.1 eq.45
  1.6 0.8 copy.8
  2.4 0.6 pad.8.cols_ref
  3.0 0.7 select_select_fusion.table_hbm
  3.7 110.9 %block_product.1 = f32[3,4,128,128]{3,2,1,0:T(8,128)} custom-call(bf16[3,16,48,128]{3,2,1,0:T(8,128)(2,1)} %bitcast.23, s32[16,8,128]{2,1,0:T(8,128)} %pad.8.cols_ref, bf16[336,128,128]{2,1,0:T(8,128)(2,1)} %bitcast.21, s32[192,128]{1,0:T(8,128)} %select_select_fusion.table_hbm), custom_call_target="tpu_custom_call" | custom-call | tf_op jit(solution)/shard_map/block_product/pallas_call | solution.py:348
  114.6 2.1 %copy.15 = f32[3,1,4,128,128]{4,3,2,1,0:T(8,128)} copy(f32[3,1,4,128,128]{4,3,2,1,0:T(8,128)} %bitcast.22) | data formatting | bytes 1572864
  (3 shorter events, 0.0 us)

commit v3 on v2

--- a/solution.py
+++ b/solution.py
@@ -19,7 +19,7 @@
 DUMMY = Z_RECVS + X_RECVS
 FAR, NEAR, DONE = 0, 1, 2
 FIRST_COL = (0, 0, 2)
-LEAD_A, LEAD_B, LEAD_C, LEAD_D = 4, 3, 2, 1
+LEAD_A, LEAD_B, LEAD_C, LEAD_D = 3, 2, 1, 0
 AHEAD = 4
 
 
@@ -269,11 +269,11 @@
             copy.start()
 
     def one_step(i, carry):
+        for lead, stage in ((LEAD_D, stage_d), (LEAD_C, stage_c), (LEAD_B, stage_b)):
+            n = i - LEAD_A + lead
+            pl.when((n >= 0) & (n < 8))(lambda stage=stage, n=n: stage(n))
         pl.when(i < 8)(lambda: stage_a(i))
         pl.when(i + AHEAD < 8)(lambda: send_blk(i + AHEAD))
-        for lead, stage in ((LEAD_B, stage_b), (LEAD_C, stage_c), (LEAD_D, stage_d)):
-            n = i - LEAD_A + lead
-            pl.when((n >= 0) & (n < 8))(lambda stage=stage, n=n: stage(n))
 
         @pl.when(i >= LEAD_A)
         def _():

time: 118 us -> 110 us (0.932)
  Pallas kernels: 111 us -> 103 us
    pallas_call x1, Pallas kernels: 111 us -> 103 us  [per_device(): pl.pallas_call(kernel, out_shape=jax.ShapeDtypeStruct((ROWS, KC, BS, BS),...]
where the time goes in v3:
time: 110 us; the launch traced here: 108 us
  Pallas kernels  103 us (94%)
  local copies, waits for them, and re-layouts  5.06 us (5%)
    pallas_call x1, Pallas kernels, per_device(): pl.pallas_call(kernel, out_shape=jax.ShapeDtypeStruct((ROWS, KC, BS, BS),...  103 us
    unnamed x4, local copies, waits for them, and re-layouts  4.32 us

profile of v3, /device:TPU:26, one launch (start us, length us, event | category | flops | bytes accessed | tf_op | source)
XLA Modules:
  0.0 108.3 jit_solution(13198164145158834460)
XLA Ops:
  0.0 0.7 copy.13
  0.7 0.8 copy.9
  1.5 0.1 eq.45
  1.6 0.8 copy.8
  2.4 0.6 pad.8.cols_ref
  3.0 0.7 select_select_fusion.table_hbm
  3.7 102.5 %block_product.1 = f32[3,4,128,128]{3,2,1,0:T(8,128)} custom-call(bf16[3,16,48,128]{3,2,1,0:T(8,128)(2,1)} %bitcast.23, s32[16,8,128]{2,1,0:T(8,128)} %pad.8.cols_ref, bf16[336,128,128]{2,1,0:T(8,128)(2,1)} %bitcast.21, s32[192,128]{1,0:T(8,128)} %select_select_fusion.table_hbm), custom_call_target="tpu_custom_call" | custom-call | tf_op jit(solution)/shard_map/block_product/pallas_call | solution.py:348
  106.3 2.1 %copy.15 = f32[3,1,4,128,128]{4,3,2,1,0:T(8,128)} copy(f32[3,1,4,128,128]{4,3,2,1,0:T(8,128)} %bitcast.22) | data formatting | bytes 1572864
  (3 shorter events, 0.0 us)
